TPU v7x, 32 devices: a whole 2x2x4 slice. The times are simulated.
32 devices in a mesh: gx: 8 (over z, y), gy: 4 (over x, core).
Axes of the slice: x: 2, y: 2, z: 4, core: 2. Of those that a mesh axis runs over, the one named last changes fastest.
Arguments:
- forward_pops: float32 [19, 64, 64, 128], P(None, 'gx', 'gy'), may hold values from 0.005 to 1, as said below
- later_adjoint: float32 [19, 64, 64, 128], P(None, 'gx', 'gy'), may hold values from -6 to 6
- design: float32 [64, 64, 128], P('gx', 'gy'), may hold values from 0 to 1
- node_type: int32 [64, 64, 128], P('gx', 'gy'), may hold values from 0 to 4, as said below
- region: int32 [64, 64, 128], P('gx', 'gy'), may hold values from 0 to 7
Outputs:
- adjoint: float32 [19, 64, 64, 128], P(None, 'gx', 'gy')
- sensitivity: float32 [64, 64, 128], P('gx', 'gy')
- objective: float32 [], replicated
- volumes: float32 [8], replicated
Inputs may be any that keep to these rules, and one draw needn't show every extreme that they name: `node_type`: 0 fluid, 1 design, 2 wall, 3 inlet, 4 outlet. `forward_pops`: positive populations.
All inputs are finite; a program needn't handle non-finite values.
Results may differ from a plain program's by a relative error of at most 0.00002.
Values sent between devices are 32-bit elements; how exact they have to be, the bound alone decides.
A program may use at most 64 MiB of HBM per device.

v0:
```python
import math

import jax
import jax.numpy as jnp
from jax import lax
from jax.sharding import PartitionSpec as P

RAD = 3
REG = 8


VELOCITY = [
    (0, 0, 0),
    (1, 0, 0),
    (-1, 0, 0),
    (0, 1, 0),
    (0, -1, 0),
    (0, 0, 1),
    (0, 0, -1),
    (1, 1, 0),
    (-1, -1, 0),
    (1, -1, 0),
    (-1, 1, 0),
    (1, 0, 1),
    (-1, 0, -1),
    (1, 0, -1),
    (-1, 0, 1),
    (0, 1, 1),
    (0, -1, -1),
    (0, 1, -1),
    (0, -1, 1),
]
WEIGHTS = [1.0 / 3.0] + [1.0 / 18.0] * 6 + [1.0 / 36.0] * 12
OPPOSITE = [0, 2, 1, 4, 3, 6, 5, 8, 7, 10, 9, 12, 11, 14, 13, 16, 15, 18, 17]
RELAXATION = 1.0 / 0.6
BRINKMAN = 0.9


def padded_2(block, sides, width):
    for axis, dim in sides:
        count = lax.axis_size(axis)
        forward = [(i, i + 1) for i in range(count - 1)]
        forward.append((count - 1, 0))
        backward = [(target, source) for source, target in forward]
        low = lax.ppermute(
            lax.slice_in_dim(block, block.shape[dim] - width, None, axis=dim), axis, forward
        )
        high = lax.ppermute(lax.slice_in_dim(block, 0, width, axis=dim), axis, backward)
        block = jnp.concatenate([low, block, high], axis=dim)
    return block


def moments(populations):
    density = populations[0]
    for i in range(1, 19):
        density = density + populations[i]
    momenta = []
    for a in range(3):
        running = jnp.zeros_like(density)
        for i in range(19):
            if VELOCITY[i][a] == 1:
                running = running + populations[i]
            elif VELOCITY[i][a] == -1:
                running = running - populations[i]
        momenta.append(running)
    return (density, momenta)


def projections(velocity):
    result = []
    for i in range(19):
        running = jnp.zeros_like(velocity[0])
        for a in range(3):
            if VELOCITY[i][a] != 0:
                running = running + VELOCITY[i][a] * velocity[a]
        result.append(running)
    return result


def rates(kind):
    return jnp.where(kind <= 1, RELAXATION, 1.0)


def collide(populations, kind, factor):
    density, momenta = moments(populations)
    plain = [m / density for m in momenta]
    velocity = [factor * p for p in plain]
    speed_sq = velocity[0] * velocity[0] + velocity[1] * velocity[1] + velocity[2] * velocity[2]
    along = projections(velocity)
    omega_cell = rates(kind)
    wall = kind == 2
    output = []
    for i in range(19):
        balance = (
            WEIGHTS[i]
            * density
            * (1.0 + 3.0 * along[i] + 4.5 * along[i] * along[i] - 1.5 * speed_sq)
        )
        relaxed = (1.0 - omega_cell) * populations[i] + omega_cell * balance
        output.append(jnp.where(wall, populations[OPPOSITE[i]], relaxed))
    return jnp.stack(output)


def adjoint_collide(incoming, populations, kind, factor):
    density, momenta = moments(populations)
    plain = [m / density for m in momenta]
    velocity = [factor * p for p in plain]
    speed_sq = velocity[0] * velocity[0] + velocity[1] * velocity[1] + velocity[2] * velocity[2]
    along = projections(velocity)
    omega_cell = rates(kind)
    wall = kind == 2
    scalar_part = jnp.zeros_like(density)
    vector_part = [jnp.zeros_like(density), jnp.zeros_like(density), jnp.zeros_like(density)]
    for j in range(19):
        weighted = WEIGHTS[j] * incoming[j]
        scalar_part = scalar_part + weighted * (
            1.0 + 3.0 * along[j] + 4.5 * along[j] * along[j] - 1.5 * speed_sq
        )
        for a in range(3):
            vector_part[a] = vector_part[a] + weighted * (
                3.0 * VELOCITY[j][a] + 9.0 * along[j] * VELOCITY[j][a] - 3.0 * velocity[a]
            )
    output = []
    for i in range(19):
        coupling = scalar_part
        for a in range(3):
            coupling = coupling + vector_part[a] * (factor * VELOCITY[i][a] - velocity[a])
        relaxed = (1.0 - omega_cell) * incoming[i] + omega_cell * coupling
        output.append(jnp.where(wall, incoming[OPPOSITE[i]], relaxed))
    inner = vector_part[0] * plain[0] + vector_part[1] * plain[1] + vector_part[2] * plain[2]
    gradient = jnp.where(wall, 0.0, omega_cell * density * inner)
    return (jnp.stack(output), gradient)


def displace(extended, sign):
    padded = jnp.pad(extended, ((0, 0), (0, 0), (0, 0), (1, 1)))
    span_x = extended.shape[1] - 2
    span_y = extended.shape[2] - 2
    span_z = extended.shape[3]
    pieces = []
    for i in range(19):
        off_x = 1 + sign * VELOCITY[i][0]
        off_y = 1 + sign * VELOCITY[i][1]
        off_z = 1 + sign * VELOCITY[i][2]
        pieces.append(
            padded[i, off_x : off_x + span_x, off_y : off_y + span_y, off_z : off_z + span_z]
        )
    return jnp.stack(pieces)


def filter_taps(padded):
    span_x = padded.shape[0] - 2 * RAD
    span_y = padded.shape[1] - 2 * RAD
    span_z = padded.shape[2] - 2 * RAD
    running = jnp.zeros((span_x, span_y, span_z), jnp.float32)
    for a in range(-RAD, RAD + 1):
        for b in range(-RAD, RAD + 1):
            for c in range(-RAD, RAD + 1):
                weight = RAD + 1 - math.sqrt(a * a + b * b + c * c)
                if weight > 0:
                    running = (
                        running
                        + weight
                        * padded[
                            RAD + a : RAD + a + span_x,
                            RAD + b : RAD + b + span_y,
                            RAD + c : RAD + c + span_z,
                        ]
                    )
    return running


def filter_norm(depth):
    block = jnp.pad(
        jnp.ones((2 * RAD + 1, 2 * RAD + 1, depth), jnp.float32), ((0, 0), (0, 0), (RAD, RAD))
    )
    return filter_taps(block)


def filter_block(field):
    extended = padded_2(field, (("gx", 0), ("gy", 1)), RAD)
    return filter_taps(jnp.pad(extended, ((0, 0), (0, 0), (RAD, RAD))))


def lattice_rim(populations):
    return padded_2(populations, (("gx", 1), ("gy", 2)), 1)


def outlet_source(kind):
    source = jnp.where(kind == 4, 1.0, 0.0)
    return jnp.stack([VELOCITY[i][0] * source for i in range(19)])


def per_device(forward_pops, later_adjoint, design, node_type, region):
    norm_field = filter_norm(design.shape[2])
    filtered = filter_block(design) / norm_field
    factor = jnp.where(node_type == 1, 1.0 - BRINKMAN * (1.0 - filtered), 1.0)
    volume_local = jnp.stack(
        [jnp.sum(jnp.where((node_type == 1) & (region == r), filtered, 0.0)) for r in range(REG)]
    )
    post = collide(forward_pops, node_type, factor)
    both = lattice_rim(jnp.concatenate([post, later_adjoint], axis=0))
    next_pops = displace(both[:19], -1)
    incoming = displace(both[19:], 1)
    middle, first_grad = adjoint_collide(incoming, next_pops, node_type, factor)
    middle = middle + outlet_source(node_type)
    incoming = displace(lattice_rim(middle), 1)
    adjoint, second_grad = adjoint_collide(incoming, forward_pops, node_type, factor)
    density, momenta = moments(next_pops)
    objective_local = jnp.sum(jnp.where(node_type == 4, momenta[0], 0.0))
    objective, volumes = lax.psum((objective_local, volume_local), ("gx", "gy"))
    raw = jnp.where(node_type == 1, BRINKMAN * (first_grad + second_grad), 0.0) / norm_field
    sensitivity = filter_block(raw)
    return (adjoint, sensitivity, objective, volumes)


def solution(mesh):
    in_specs = (
        P(None, "gx", "gy", None),
        P(None, "gx", "gy", None),
        P("gx", "gy", None),
        P("gx", "gy", None),
        P("gx", "gy", None),
    )
    out_specs = (P(None, "gx", "gy", None), P("gx", "gy", None), P(), P())
    return jax.shard_map(
        per_device, mesh=mesh, in_specs=in_specs, out_specs=out_specs, check_vma=False
    )
```

profile of v0, /device:TPU:1, one launch (start us, length us, event | category | flops | bytes accessed | tf_op | source)
XLA Modules:
  0.0 129.6 jit_solution(746766798177973993)
XLA Ops:
  0.6 0.8 fusion.991
  1.4 2.1 %collective-permute-start = (f32[3,16,128]{2,1,0:T(8,128)S(1)}, f32[3,16,128]{2,1,0:T(8,128)S(1)}, u32[]{:S(2)}, u32[]{:S(2)}) collective-permute-start(f32[3,16,128]{2,1,0:T(8,128)S(1)} %get-tuple-element.162), channel_id=1, source_target_pairs={{0,4},{4,8},{8,12},{12,16},{16,20},{20,24},{24,28},{28,0},{1,5},{5... | collective-permute-start | bytes 73736 | tf_op jit(solution)/shard_map/ppermute | solution.py:45
  3.5 3.1 %collective-permute-start.1 = (f32[3,16,128]{2,1,0:T(8,128)S(1)}, f32[3,16,128]{2,1,0:T(8,128)S(1)}, u32[]{:S(2)}, u32[]{:S(2)}) collective-permute-start(f32[3,16,128]{2,1,0:T(8,128)S(1)} %get-tuple-element.161), channel_id=1, source_target_pairs={{4,0},{8,4},{12,8},{16,12},{20,16},{24,20},{28,24},{0,28},{5,1},{9... | collective-permute-start | bytes 73736 | tf_op jit(solution)/shard_map/ppermute | solution.py:48
  6.5 1.3 collective-permute-done
  7.8 0.9 constant_dynamic-update-slice_fusion.3
  8.7 2.8 %collective-permute-start.2 = (f32[14,3,128]{2,1,0:T(4,128)S(1)}, f32[14,3,128]{2,1,0:T(4,128)S(1)}, u32[]{:S(2)}, u32[]{:S(2)}) collective-permute-start(f32[14,3,128]{2,1,0:T(4,128)S(1)} %get-tuple-element.153), channel_id=1, source_target_pairs={{0,1},{1,2},{2,3},{3,0},{4,5},{5,6},{6,7},{7,4},{8,9},{9,10},{10,1... | collective-permute-start | bytes 64520 | tf_op jit(solution)/shard_map/ppermute | solution.py:45
  11.5 0.3 add_add_fusion.1
  11.8 0.6 collective-permute-done.2
  12.5 2.3 %collective-permute-done.3 = f32[14,3,128]{2,1,0:T(4,128)S(1)} collective-permute-done((f32[14,3,128]{2,1,0:T(4,128)S(1)}, f32[14,3,128]{2,1,0:T(4,128)S(1)}, u32[]{:S(2)}, u32[]{:S(2)}) %collective-permute-start.3) | collective-permute-done | bytes 21536 | tf_op jit(solution)/shard_map/ppermute | solution.py:48
  14.8 0.2 select_maximum_fusion.8
  15.0 0.4 slice_multiply_fusion.399
  15.4 0.1 slice_multiply_fusion.398
  15.7 3.1 %fusion.254 = f32[8,16,128]{2,1,0:T(8,128)S(1)} fusion(f32[8,16,128]{2,1,0:T(8,128)S(1)} %div.35, f32[8,16,128]{2,1,0:T(8,128)S(1)} %broadcast.809, f32[14,16,128]{2,1,0:T(8,128)S(1)} %get-tuple-element.166, f32[14,3,128]{2,1,0:T(4,128)S(1)} %collective-permute-done.3, f32[8,16,128]{2,1,0:T(8,128)S(1)} %broadcast.806, ...), kind=kLoop, calls=%fused_computation.554 | loop fusion | flops 7995392 | bytes 15034368 | tf_op jit(solution)/shard_map/div | solution.py:196
  18.9 0.8 select_reduce_fusion
  19.7 0.8 constant_dynamic-update-slice_fusion.26
  21.5 1.0 copy-done.1
  22.5 0.1 constant_dynamic-update-slice_fusion.7
  22.7 0.1 collective-permute-start.4
  22.8 4.1 %collective-permute-start.5 = (f32[38,1,16,128]{3,2,1,0:T(8,128)S(1)}, f32[38,1,16,128]{3,2,1,0:T(8,128)S(1)}, u32[]{:S(2)}, u32[]{:S(2)}) collective-permute-start(f32[38,1,16,128]{3,2,1,0:T(8,128)S(1)} %get-tuple-element.108), channel_id=1, source_target_pairs={{4,0},{8,4},{12,8},{16,12},{20,16},{24,20},{28,24},{0,28},{5,1},{9... | collective-permute-start | bytes 933896 | tf_op jit(solution)/shard_map/ppermute | solution.py:48
  26.9 9.1 %collective-permute-done.4 = f32[38,1,16,128]{3,2,1,0:T(8,128)S(1)} collective-permute-done((f32[38,1,16,128]{3,2,1,0:T(8,128)S(1)}, f32[38,1,16,128]{3,2,1,0:T(8,128)S(1)}, u32[]{:S(2)}, u32[]{:S(2)}) %collective-permute-start.4) | collective-permute-done | bytes 311328 | tf_op jit(solution)/shard_map/ppermute | solution.py:45
  36.0 2.2 %collective-permute-done.5 = f32[38,1,16,128]{3,2,1,0:T(8,128)S(1)} collective-permute-done((f32[38,1,16,128]{3,2,1,0:T(8,128)S(1)}, f32[38,1,16,128]{3,2,1,0:T(8,128)S(1)}, u32[]{:S(2)}, u32[]{:S(2)}) %collective-permute-start.5) | collective-permute-done | bytes 311328 | tf_op jit(solution)/shard_map/ppermute | solution.py:48
  38.2 0.3 pad_maximum_fusion.3
  38.5 1.2 collective-permute-start.6
  39.7 3.5 %collective-permute-done.6 = f32[38,10,1,128]{3,2,1,0:T(1,128)S(1)} collective-permute-done((f32[38,10,1,128]{3,2,1,0:T(1,128)S(1)}, f32[38,10,1,128]{3,2,1,0:T(1,128)S(1)}, u32[]{:S(2)}, u32[]{:S(2)}) %collective-permute-start.6) | collective-permute-done | bytes 194592 | tf_op jit(solution)/shard_map/ppermute | solution.py:45
  43.2 2.3 %collective-permute-done.7 = f32[38,10,1,128]{3,2,1,0:T(1,128)S(1)} collective-permute-done((f32[38,10,1,128]{3,2,1,0:T(1,128)S(1)}, f32[38,10,1,128]{3,2,1,0:T(1,128)S(1)}, u32[]{:S(2)}, u32[]{:S(2)}) %collective-permute-start.7) | collective-permute-done | bytes 194592 | tf_op jit(solution)/shard_map/ppermute | solution.py:48
  45.4 0.9 pad_maximum_fusion
  46.4 0.3 fusion.986
  46.7 0.7 select_reduce_fusion.8
  47.8 1.7 %constant_dynamic-update-slice_fusion.45 = (f32[19,8,16,128]{3,2,1,0:T(8,128)S(1)}, f32[8,16,128]{2,1,0:T(8,128)S(1)}, f32[8,16,128]{2,1,0:T(8,128)S(1)}, f32[8,...) fusion(pred[8,16,128]{2,1,0:T(8,128)(4,1)S(1)} %get-tuple-eleme, ...), kind=kLoop, calls=%fused_computation.274 | loop fusion | flops 8601599 | bytes 9265152
  49.7 0.1 constant_dynamic-update-slice_fusion.40
  49.9 0.1 constant_dynamic-update-slice_fusion.39
  50.1 0.1 constant_dynamic-update-slice_fusion.34
  50.3 0.1 constant_dynamic-update-slice_fusion.33
  50.4 0.1 constant_dynamic-update-slice_fusion.32
  50.5 0.1 constant_dynamic-update-slice_fusion.31
  50.6 0.1 constant_dynamic-update-slice_fusion.30
  50.7 0.1 constant_dynamic-update-slice_fusion.29
  50.8 0.1 constant_dynamic-update-slice_fusion.28
  50.9 0.1 constant_dynamic-update-slice_fusion.27
  51.0 0.2 add.4920
  51.3 2.8 %collective-permute-start.8 = (f32[19,1,16,128]{3,2,1,0:T(8,128)S(1)}, f32[19,1,16,128]{3,2,1,0:T(8,128)S(1)}, u32[]{:S(2)}, u32[]{:S(2)}) collective-permute-start(f32[19,1,16,128]{3,2,1,0:T(8,128)S(1)} %get-tuple-element.112), channel_id=1, source_target_pairs={{4,0},{8,4},{12,8},{16,12},{20,16},{24,20},{28,24},{0,28},{5,1},{9... | collective-permute-start | bytes 466952 | tf_op jit(solution)/shard_map/ppermute | solution.py:48
  54.1 3.5 %collective-permute-done.8 = f32[19,1,16,128]{3,2,1,0:T(8,128)S(1)} collective-permute-done((f32[19,1,16,128]{3,2,1,0:T(8,128)S(1)}, f32[19,1,16,128]{3,2,1,0:T(8,128)S(1)}, u32[]{:S(2)}, u32[]{:S(2)}) %collective-permute-start.8) | collective-permute-done | bytes 155680 | tf_op jit(solution)/shard_map/ppermute | solution.py:48
  57.5 4.6 %collective-permute-done.9 = f32[19,1,16,128]{3,2,1,0:T(8,128)S(1)} collective-permute-done((f32[19,1,16,128]{3,2,1,0:T(8,128)S(1)}, f32[19,1,16,128]{3,2,1,0:T(8,128)S(1)}, u32[]{:S(2)}, u32[]{:S(2)}) %collective-permute-start.9) | collective-permute-done | bytes 155680 | tf_op jit(solution)/shard_map/ppermute | solution.py:45
  62.1 0.8 pad_maximum_fusion.5
  62.9 1.1 collective-permute-start.10
  64.0 1.4 %collective-permute-start.11 = (f32[19,10,1,128]{3,2,1,0:T(1,128)}, f32[19,10,1,128]{3,2,1,0:T(1,128)S(1)}, u32[]{:S(2)}, u32[]{:S(2)}) collective-permute-start(f32[19,10,1,128]{3,2,1,0:T(1,128)} %get-tuple-element.109), channel_id=1, source_target_pairs={{0,1},{1,2},{2,3},{3,0},{4,5},{5,6},{6,7},{7,4},{8,9},{9,10},{10,1... | collective-permute-start | bytes 291848 | tf_op jit(solution)/shard_map/ppermute | solution.py:45
  65.4 5.7 %stack.303 = f32[8]{0:T(128)} concatenate(f32[1]{0:T(128)} %bitcast.135, f32[1]{0:T(128)} %bitcast.136, f32[1]{0:T(128)} %bitcast.137, f32[1]{0:T(128)} %bitcast.138, f32[1]{0:T(128)} %bitcast.139, f32[1]{0:T(128)} %bitcast.140, f32[1]{0:T(128)} %bitcast.141, f32[1]{0:T(128)} %bitcast.142), dimensions={0} | concatenate | bytes 64 | tf_op jit(solution)/shard_map/stack | solution.py:198
  71.1 35.5 %all-reduce.6 = (f32[]{:T(128)}, f32[8]{0:T(128)}) all-reduce(f32[]{:T(128)} %get-tuple-element.15, f32[8]{0:T(128)} %stack.303), channel_id=1, replica_groups=mesh['gx'=8,'gy'=4] {'gx','gy'}, use_global_device_ids=true, to_apply=%region_1.2 | all-reduce | flops 9 | bytes 72 | tf_op jit(solution)/shard_map/psum | solution.py:211
  106.7 4.3 %select_maximum_fusion = f32[19,10,18,130]{3,2,1,0:T(8,128)S(1)} fusion(f32[19,10,1,128]{3,2,1,0:T(1,128)S(1)} %collective-permute-done.10, f32[19,10,1,128]{3,2,1,0:T(1,128)S(1)} %collective-permute-done.11, f32[19,1,16,128]{3,2,1,0:T(8,128)S(1)} %collective-permute-done.8, f32[19,8,16,128]{3,2,1,0:T(8,128)S(1)} %add.4920, ...), kind=kLoop, calls=%fused_computation.22 | loop fusion | flops 5335200 | bytes 3529440 | tf_op jit(solution)/shard_map/concatenate | solution.py:49
  111.0 1.0 broadcast_multiply_fusion.1
  112.0 2.0 %collective-permute-start.12 = (f32[3,16,128]{2,1,0:T(8,128)S(1)}, f32[3,16,128]{2,1,0:T(8,128)S(1)}, u32[]{:S(2)}, u32[]{:S(2)}) collective-permute-start(f32[3,16,128]{2,1,0:T(8,128)S(1)} %get-tuple-element.155), channel_id=1, source_target_pairs={{0,4},{4,8},{8,12},{12,16},{16,20},{20,24},{24,28},{28,0},{1,5},{5... | collective-permute-start | bytes 73736 | tf_op jit(solution)/shard_map/ppermute | solution.py:45
  114.0 2.3 %collective-permute-start.13 = (f32[3,16,128]{2,1,0:T(8,128)S(1)}, f32[3,16,128]{2,1,0:T(8,128)S(1)}, u32[]{:S(2)}, u32[]{:S(2)}) collective-permute-start(f32[3,16,128]{2,1,0:T(8,128)S(1)} %get-tuple-element.156), channel_id=1, source_target_pairs={{4,0},{8,4},{12,8},{16,12},{20,16},{24,20},{28,24},{0,28},{5,1},{9... | collective-permute-start | bytes 73736 | tf_op jit(solution)/shard_map/ppermute | solution.py:48
  116.2 0.5 constant_dynamic-update-slice_fusion.83
  117.0 0.1 constant_dynamic-update-slice_fusion.78
  117.3 0.1 constant_dynamic-update-slice_fusion.72
  117.6 0.1 constant_dynamic-update-slice_fusion.69
  117.7 0.1 constant_dynamic-update-slice_fusion.68
  118.0 3.8 %collective-permute-start.14 = (f32[14,3,128]{2,1,0:T(4,128)S(1)}, f32[14,3,128]{2,1,0:T(4,128)S(1)}, u32[]{:S(2)}, u32[]{:S(2)}) collective-permute-start(f32[14,3,128]{2,1,0:T(4,128)S(1)} %get-tuple-element.151), channel_id=1, source_target_pairs={{0,1},{1,2},{2,3},{3,0},{4,5},{5,6},{6,7},{7,4},{8,9},{9,10},{10,1... | collective-permute-start | bytes 64520 | tf_op jit(solution)/shard_map/ppermute | solution.py:45
  122.0 0.9 collective-permute-done.14
  122.9 2.2 %collective-permute-done.15 = f32[14,3,128]{2,1,0:T(4,128)S(1)} collective-permute-done((f32[14,3,128]{2,1,0:T(4,128)S(1)}, f32[14,3,128]{2,1,0:T(4,128)S(1)}, u32[]{:S(2)}, u32[]{:S(2)}) %collective-permute-start.15) | collective-permute-done | bytes 21536 | tf_op jit(solution)/shard_map/ppermute | solution.py:48
  125.2 0.2 select_maximum_fusion.4
  125.4 0.2 slice_multiply_fusion.176
  125.7 0.6 fusion.871
  126.2 3.3 %fusion.735 = f32[8,16,128]{2,1,0:T(8,128)} fusion(f32[8,16,128]{2,1,0:T(8,128)S(1)} %broadcast.806, f32[14,22,134]{2,1,0:T(8,128)S(1)} %select_maximum_fusion.4, f32[8,16,128]{2,1,0:T(8,128)S(1)} %broadcast.807, f32[14,19,128]{2,1,0:T(8,128)S(1)} %get-tuple-element.150, f32[8,16,128]{2,1,0:T(8,128)S(1)} %broadcast.808, f32[8,16,128]{2,1,0:T(8,128)S(1)} %broadcast.809, ...), kind=kLoop, calls=%fused_computation.1036 | loop fusion | flops 6438912 | bytes 14598144 | tf_op jit(solution)/shard_map/add | solution.py:162
  (111 shorter events, 2.7 us)
Async XLA Ops:
  1.4 6.4 %collective-permute-start = (f32[3,16,128]{2,1,0:T(8,128)S(1)}, f32[3,16,128]{2,1,0:T(8,128)S(1)}, u32[]{:S(2)}, u32[]{:S(2)}) collective-permute-start(f32[3,16,128]{2,1,0:T(8,128)S(1)} %get-tuple-element.162), channel_id=1, source_target_pairs={{0,4},{4,8},{8,12},{12,16},{16,20},{20,24},{24,28},{28,0},{1,5},{5... | collective-permute-start | bytes 73736 | tf_op jit(solution)/shard_map/ppermute | solution.py:45
  3.5 5.2 %collective-permute-start.1 = (f32[3,16,128]{2,1,0:T(8,128)S(1)}, f32[3,16,128]{2,1,0:T(8,128)S(1)}, u32[]{:S(2)}, u32[]{:S(2)}) collective-permute-start(f32[3,16,128]{2,1,0:T(8,128)S(1)} %get-tuple-element.161), channel_id=1, source_target_pairs={{4,0},{8,4},{12,8},{16,12},{20,16},{24,20},{28,24},{0,28},{5,1},{9... | collective-permute-start | bytes 73736 | tf_op jit(solution)/shard_map/ppermute | solution.py:48
  8.7 3.7 %collective-permute-start.2 = (f32[14,3,128]{2,1,0:T(4,128)S(1)}, f32[14,3,128]{2,1,0:T(4,128)S(1)}, u32[]{:S(2)}, u32[]{:S(2)}) collective-permute-start(f32[14,3,128]{2,1,0:T(4,128)S(1)} %get-tuple-element.153), channel_id=1, source_target_pairs={{0,1},{1,2},{2,3},{3,0},{4,5},{5,6},{6,7},{7,4},{8,9},{9,10},{10,1... | collective-permute-start | bytes 64520 | tf_op jit(solution)/shard_map/ppermute | solution.py:45
  11.5 3.3 %collective-permute-start.3 = (f32[14,3,128]{2,1,0:T(4,128)S(1)}, f32[14,3,128]{2,1,0:T(4,128)S(1)}, u32[]{:S(2)}, u32[]{:S(2)}) collective-permute-start(f32[14,3,128]{2,1,0:T(4,128)S(1)} %get-tuple-element.154), channel_id=1, source_target_pairs={{1,0},{2,1},{3,2},{0,3},{5,4},{6,5},{7,6},{4,7},{9,8},{10,9},{11,1... | collective-permute-start | bytes 64520 | tf_op jit(solution)/shard_map/ppermute | solution.py:48
  11.8 3.7 %copy-start.8 = (f32[128]{0:T(128)}, f32[128]{0:T(128)S(1)}, u32[]{:S(2)}) copy-start(f32[128]{0:T(128)S(1)} %add_add_fusion.1) | copy-start | bytes 1540
  15.7 3.1 %copy-start.2 = (s32[8,16,128]{2,1,0:T(8,128)S(1)}, s32[8,16,128]{2,1,0:T(8,128)}, u32[]{:S(2)}) copy-start(s32[8,16,128]{2,1,0:T(8,128)} %param.8) | copy-start | bytes 196612
  15.7 3.1 %copy-start.6 = (s32[8,16,128]{2,1,0:T(8,128)S(1)}, s32[8,16,128]{2,1,0:T(8,128)}, u32[]{:S(2)}) copy-start(s32[8,16,128]{2,1,0:T(8,128)} %param.9) | copy-start | bytes 196612
  15.7 3.9 %copy-start = (f32[19,8,16,128]{3,2,1,0:T(8,128)S(1)}, f32[19,8,16,128]{3,2,1,0:T(8,128)}, u32[]{:S(2)}) copy-start(f32[19,8,16,128]{3,2,1,0:T(8,128)} %param.5) | copy-start | bytes 3735556
  19.7 0.9 copy-start.4
  21.2 1.3 %copy-start.1 = (f32[19,8,16,128]{3,2,1,0:T(8,128)S(1)}, f32[19,8,16,128]{3,2,1,0:T(8,128)}, u32[]{:S(2)}) copy-start(f32[19,8,16,128]{3,2,1,0:T(8,128)} %param.6) | copy-start | bytes 3735556
  22.7 13.3 %collective-permute-start.4 = (f32[38,1,16,128]{3,2,1,0:T(8,128)S(1)}, f32[38,1,16,128]{3,2,1,0:T(8,128)S(1)}, u32[]{:S(2)}, u32[]{:S(2)}) collective-permute-start(f32[38,1,16,128]{3,2,1,0:T(8,128)S(1)} %get-tuple-element.107), channel_id=1, source_target_pairs={{0,4},{4,8},{8,12},{12,16},{16,20},{20,24},{24,28},{28,0},{1,5},{5... | collective-permute-start | bytes 933896 | tf_op jit(solution)/shard_map/ppermute | solution.py:45
  22.8 15.4 %collective-permute-start.5 = (f32[38,1,16,128]{3,2,1,0:T(8,128)S(1)}, f32[38,1,16,128]{3,2,1,0:T(8,128)S(1)}, u32[]{:S(2)}, u32[]{:S(2)}) collective-permute-start(f32[38,1,16,128]{3,2,1,0:T(8,128)S(1)} %get-tuple-element.108), channel_id=1, source_target_pairs={{4,0},{8,4},{12,8},{16,12},{20,16},{24,20},{28,24},{0,28},{5,1},{9... | collective-permute-start | bytes 933896 | tf_op jit(solution)/shard_map/ppermute | solution.py:48
  38.5 4.7 %collective-permute-start.6 = (f32[38,10,1,128]{3,2,1,0:T(1,128)S(1)}, f32[38,10,1,128]{3,2,1,0:T(1,128)S(1)}, u32[]{:S(2)}, u32[]{:S(2)}) collective-permute-start(f32[38,10,1,128]{3,2,1,0:T(1,128)S(1)} %get-tuple-element.105), channel_id=1, source_target_pairs={{0,1},{1,2},{2,3},{3,0},{4,5},{5,6},{6,7},{7,4},{8,9},{9,10},{10,1... | collective-permute-start | bytes 583688 | tf_op jit(solution)/shard_map/ppermute | solution.py:45
  39.7 5.7 %collective-permute-start.7 = (f32[38,10,1,128]{3,2,1,0:T(1,128)S(1)}, f32[38,10,1,128]{3,2,1,0:T(1,128)S(1)}, u32[]{:S(2)}, u32[]{:S(2)}) collective-permute-start(f32[38,10,1,128]{3,2,1,0:T(1,128)S(1)} %get-tuple-element.106), channel_id=1, source_target_pairs={{1,0},{2,1},{3,2},{0,3},{5,4},{6,5},{7,6},{4,7},{9,8},{10,9},{11,1... | collective-permute-start | bytes 583688 | tf_op jit(solution)/shard_map/ppermute | solution.py:48
  51.3 6.2 %collective-permute-start.8 = (f32[19,1,16,128]{3,2,1,0:T(8,128)S(1)}, f32[19,1,16,128]{3,2,1,0:T(8,128)S(1)}, u32[]{:S(2)}, u32[]{:S(2)}) collective-permute-start(f32[19,1,16,128]{3,2,1,0:T(8,128)S(1)} %get-tuple-element.112), channel_id=1, source_target_pairs={{4,0},{8,4},{12,8},{16,12},{20,16},{24,20},{28,24},{0,28},{5,1},{9... | collective-permute-start | bytes 466952 | tf_op jit(solution)/shard_map/ppermute | solution.py:48
  54.0 8.0 %collective-permute-start.9 = (f32[19,1,16,128]{3,2,1,0:T(8,128)S(1)}, f32[19,1,16,128]{3,2,1,0:T(8,128)S(1)}, u32[]{:S(2)}, u32[]{:S(2)}) collective-permute-start(f32[19,1,16,128]{3,2,1,0:T(8,128)S(1)} %get-tuple-element.111), channel_id=1, source_target_pairs={{0,4},{4,8},{8,12},{12,16},{16,20},{20,24},{24,28},{28,0},{1,5},{5... | collective-permute-start | bytes 466952 | tf_op jit(solution)/shard_map/ppermute | solution.py:45
  62.9 43.8 %collective-permute-start.10 = (f32[19,10,1,128]{3,2,1,0:T(1,128)}, f32[19,10,1,128]{3,2,1,0:T(1,128)S(1)}, u32[]{:S(2)}, u32[]{:S(2)}) collective-permute-start(f32[19,10,1,128]{3,2,1,0:T(1,128)} %get-tuple-element.110), channel_id=1, source_target_pairs={{1,0},{2,1},{3,2},{0,3},{5,4},{6,5},{7,6},{4,7},{9,8},{10,9},{11,1... | collective-permute-start | bytes 291848 | tf_op jit(solution)/shard_map/ppermute | solution.py:48
  64.0 42.7 %collective-permute-start.11 = (f32[19,10,1,128]{3,2,1,0:T(1,128)}, f32[19,10,1,128]{3,2,1,0:T(1,128)S(1)}, u32[]{:S(2)}, u32[]{:S(2)}) collective-permute-start(f32[19,10,1,128]{3,2,1,0:T(1,128)} %get-tuple-element.109), channel_id=1, source_target_pairs={{0,1},{1,2},{2,3},{3,0},{4,5},{5,6},{6,7},{7,4},{8,9},{9,10},{10,1... | collective-permute-start | bytes 291848 | tf_op jit(solution)/shard_map/ppermute | solution.py:45
  106.6 4.3 %copy-start.3 = (f32[8,16,128]{2,1,0:T(8,128)S(1)}, f32[8,16,128]{2,1,0:T(8,128)}, u32[]{:S(2)}) copy-start(f32[8,16,128]{2,1,0:T(8,128)} %get-tuple-element.96) | copy-start | bytes 196612
  106.6 4.3 %copy-start.5 = (pred[8,16,128]{2,1,0:T(8,128)(4,1)S(1)}, pred[8,16,128]{2,1,0:T(8,128)(4,1)}, u32[]{:S(2)}) copy-start(pred[8,16,128]{2,1,0:T(8,128)(4,1)} %copy-done.4) | copy-start | bytes 49156
  106.6 4.3 %copy-start.9 = (f32[128]{0:T(128)S(1)}, f32[128]{0:T(128)}, u32[]{:S(2)}) copy-start(f32[128]{0:T(128)} %copy-done.8) | copy-start | bytes 1540
  112.0 6.0 %collective-permute-start.12 = (f32[3,16,128]{2,1,0:T(8,128)S(1)}, f32[3,16,128]{2,1,0:T(8,128)S(1)}, u32[]{:S(2)}, u32[]{:S(2)}) collective-permute-start(f32[3,16,128]{2,1,0:T(8,128)S(1)} %get-tuple-element.155), channel_id=1, source_target_pairs={{0,4},{4,8},{8,12},{12,16},{16,20},{20,24},{24,28},{28,0},{1,5},{5... | collective-permute-start | bytes 73736 | tf_op jit(solution)/shard_map/ppermute | solution.py:45
  114.0 4.0 %collective-permute-start.13 = (f32[3,16,128]{2,1,0:T(8,128)S(1)}, f32[3,16,128]{2,1,0:T(8,128)S(1)}, u32[]{:S(2)}, u32[]{:S(2)}) collective-permute-start(f32[3,16,128]{2,1,0:T(8,128)S(1)} %get-tuple-element.156), channel_id=1, source_target_pairs={{4,0},{8,4},{12,8},{16,12},{20,16},{24,20},{28,24},{0,28},{5,1},{9... | collective-permute-start | bytes 73736 | tf_op jit(solution)/shard_map/ppermute | solution.py:48
  118.0 4.9 %collective-permute-start.14 = (f32[14,3,128]{2,1,0:T(4,128)S(1)}, f32[14,3,128]{2,1,0:T(4,128)S(1)}, u32[]{:S(2)}, u32[]{:S(2)}) collective-permute-start(f32[14,3,128]{2,1,0:T(4,128)S(1)} %get-tuple-element.151), channel_id=1, source_target_pairs={{0,1},{1,2},{2,3},{3,0},{4,5},{5,6},{6,7},{7,4},{8,9},{9,10},{10,1... | collective-permute-start | bytes 64520 | tf_op jit(solution)/shard_map/ppermute | solution.py:45
  121.9 3.3 %collective-permute-start.15 = (f32[14,3,128]{2,1,0:T(4,128)S(1)}, f32[14,3,128]{2,1,0:T(4,128)S(1)}, u32[]{:S(2)}, u32[]{:S(2)}) collective-permute-start(f32[14,3,128]{2,1,0:T(4,128)S(1)} %get-tuple-element.152), channel_id=1, source_target_pairs={{1,0},{2,1},{3,2},{0,3},{5,4},{6,5},{7,6},{4,7},{9,8},{10,9},{11,1... | collective-permute-start | bytes 64520 | tf_op jit(solution)/shard_map/ppermute | solution.py:48
  122.0 3.7 %copy-start.7 = (f32[19,8,16,128]{3,2,1,0:T(8,128)}, f32[19,8,16,128]{3,2,1,0:T(8,128)S(1)}, u32[]{:S(2)}) copy-start(f32[19,8,16,128]{3,2,1,0:T(8,128)S(1)} %constant_dynamic-update-slice_fusion.65) | copy-start | bytes 3735556
where the time goes:
time: 130 us
  blocking collectives  35.5 us (27%)
  waiting for transfers between devices  32.5 us (25%)
  starting transfers between devices  26.6 us (20%)
  other arithmetic  25.4 us (20%)
  local copies, waits for them, and re-layouts  8.11 us (6%)
  between operations  1.41 us (1%)
    psum x1, blocking collectives, per_device(): objective, volumes = lax.psum((objective_local, volume_local), ('gx', 'gy'))  35.5 us
    ppermute x8, waiting for transfers between devices, padded_2(): lax.ppermute(lax.slice_in_dim(block, block.shape[dim] - width, None, axis...  20 us
    ppermute x8, starting transfers between devices, padded_2(): lax.ppermute(lax.slice_in_dim(block, block.shape[dim] - width, None, axis...  13.3 us
    ppermute x8, starting transfers between devices, padded_2(): lax.ppermute(lax.slice_in_dim(block, 0, width, axis=dim), axis, backward)  13.3 us
    ppermute x8, waiting for transfers between devices, padded_2(): lax.ppermute(lax.slice_in_dim(block, 0, width, axis=dim), axis, backward)  12.5 us
    concatenate x7, other arithmetic, padded_2(): block = jnp.concatenate([low, block, high], axis=dim)  7.36 us
    unnamed x73, other arithmetic  6.69 us
    another operation x1, local copies, waits for them, and re-layouts, per_device(): jnp.stack([jnp.sum(jnp.where((node_type == 1) & (region == r), filtered,...  5.7 us
  transfers between devices with their start and end apart: 16, of which 11 were waited for; matrix products, arithmetic and copies ran while one was open for 7% of the time, Pallas kernels for 0%

commit v1 on v0

v1 whole, which is shorter than its diff:
```python
import functools
import math

import jax
import jax.numpy as jnp
from jax import lax
from jax.experimental import pallas as pl
from jax.experimental.pallas import tpu as pltpu
from jax.sharding import PartitionSpec as P

RAD = 3
REG = 8
MESH = pl.DeviceIdType.MESH

VELOCITY = [
    (0, 0, 0),
    (1, 0, 0),
    (-1, 0, 0),
    (0, 1, 0),
    (0, -1, 0),
    (0, 0, 1),
    (0, 0, -1),
    (1, 1, 0),
    (-1, -1, 0),
    (1, -1, 0),
    (-1, 1, 0),
    (1, 0, 1),
    (-1, 0, -1),
    (1, 0, -1),
    (-1, 0, 1),
    (0, 1, 1),
    (0, -1, -1),
    (0, 1, -1),
    (0, -1, 1),
]
W0, W1, W2 = 1.0 / 3.0, 1.0 / 18.0, 1.0 / 36.0
PAIRS = [1, 3, 5, 7, 9, 11, 13, 15, 17]
OPPOSITE = [0, 2, 1, 4, 3, 6, 5, 8, 7, 10, 9, 12, 11, 14, 13, 16, 15, 18, 17]
RELAXATION = 1.0 / 0.6
BRINKMAN = 0.9

DIRS = [(1, 0), (-1, 0), (0, 1), (0, -1), (1, 1), (-1, -1), (1, -1), (-1, 1)]
ROWS = 8
POST, LATER, MIDDLE = 0, 1, 2
DESIGN, RAW = 3, 4


def weight(a, b, c):
    return max(RAD + 1 - math.sqrt(a * a + b * b + c * c), 0.0)


def crossing(direction, sign):
    return [
        i
        for i in range(19)
        if all(
            direction[a] == 0 or sign * VELOCITY[i][a] == direction[a] for a in range(2)
        )
    ]


def lanes(shape):
    return lax.broadcasted_iota(jnp.int32, shape, len(shape) - 1)


def shifted(value, offset):
    if offset == 0:
        return value
    depth = value.shape[-1]
    z = lanes(value.shape)
    rolled = pltpu.roll(value, (-offset) % depth, value.ndim - 1)
    inside = z < depth - offset if offset > 0 else z >= -offset
    return jnp.where(inside, rolled, 0.0)


def inverse_norm(shape):
    depth = shape[-1]
    z = lanes(shape)
    span = range(-RAD, RAD + 1)
    norm = jnp.zeros(shape, jnp.float32)
    for c in span:
        layer = sum(weight(a, b, c) for a in span for b in span)
        inside = (z + c >= 0) & (z + c < depth)
        norm = norm + jnp.where(inside, layer, 0.0)
    return 1.0 / norm


def filter_taps(field, x, y):
    classes = {}
    for a in range(-RAD, RAD + 1):
        for b in range(-RAD, RAD + 1):
            if weight(a, b, 0) > 0:
                value = field[x + RAD + a, ROWS + y + b : 2 * ROWS + y + b, :]
                key = a * a + b * b
                classes[key] = classes[key] + value if key in classes else value
    result = None
    for c in range(RAD + 1):
        layer = None
        for key, value in classes.items():
            w = max(RAD + 1 - math.sqrt(key + c * c), 0.0)
            if w > 0:
                layer = w * value if layer is None else layer + w * value
        if c == 0:
            result = layer
        else:
            result = result + shifted(layer, c) + shifted(layer, -c)
    return result


def pairs_of(p):
    return (
        {i: p[i] + p[i + 1] for i in PAIRS},
        {i: p[i] - p[i + 1] for i in PAIRS},
    )


def moments(p):
    even, odd = pairs_of(p)
    density = p[0] + (
        ((even[1] + even[3]) + (even[5] + even[7]))
        + ((even[9] + even[11]) + (even[13] + (even[15] + even[17])))
    )
    momenta = [
        (odd[1] + odd[7]) + (odd[9] + (odd[11] + odd[13])),
        (odd[3] + odd[7]) + (odd[15] + odd[17] - odd[9]),
        (odd[5] + odd[11]) + (odd[15] - odd[13] - odd[17]),
    ]
    return density, momenta


def along(i, u):
    total = None
    for a in range(3):
        if VELOCITY[i][a] != 0:
            if total is None:
                total = u[a]
            elif VELOCITY[i][a] > 0:
                total = total + u[a]
            else:
                total = total - u[a]
    return total


def rates(kind):
    return jnp.where(kind <= 1, RELAXATION, 1.0)


def collide(p, density, plain, kind, factor):
    u = [factor * v for v in plain]
    base = 1.0 - 1.5 * (u[0] * u[0] + u[1] * u[1] + u[2] * u[2])
    omega = rates(kind)
    keep = 1.0 - omega
    wall = kind == 2
    scale = omega * density
    scale1 = W1 * scale
    scale2 = W2 * scale
    out = [None] * 19
    out[0] = jnp.where(wall, p[0], keep * p[0] + (W0 * scale) * base)
    for i in PAIRS:
        c_u = along(i, u)
        s = scale1 if i < 7 else scale2
        even = s * (base + 4.5 * c_u * c_u)
        odd = s * (3.0 * c_u)
        out[i] = jnp.where(wall, p[i + 1], keep * p[i] + (even + odd))
        out[i + 1] = jnp.where(wall, p[i], keep * p[i + 1] + (even - odd))
    return out


def adjoint_parts(m, plain, factor):
    u = [factor * v for v in plain]
    even, odd = pairs_of(m)
    total = W0 * m[0] + W1 * (even[1] + even[3] + even[5])
    e79, e1113, e1517 = even[7] + even[9], even[11] + even[13], even[15] + even[17]
    total = total + W2 * (e79 + e1113 + e1517)
    first = [
        W1 * odd[1] + W2 * ((odd[7] + odd[9]) + (odd[11] + odd[13])),
        W1 * odd[3] + W2 * ((odd[7] - odd[9]) + (odd[15] + odd[17])),
        W1 * odd[5] + W2 * ((odd[11] - odd[13]) + (odd[15] - odd[17])),
    ]
    xx = W1 * even[1] + W2 * (e79 + e1113)
    yy = W1 * even[3] + W2 * (e79 + e1517)
    zz = W1 * even[5] + W2 * (e1113 + e1517)
    xy = W2 * (even[7] - even[9])
    xz = W2 * (even[11] - even[13])
    yz = W2 * (even[15] - even[17])
    second = [
        xx * u[0] + xy * u[1] + xz * u[2],
        xy * u[0] + yy * u[1] + yz * u[2],
        xz * u[0] + yz * u[1] + zz * u[2],
    ]

    def dot(p, q):
        return p[0] * q[0] + p[1] * q[1] + p[2] * q[2]

    scalar = total * (1.0 - 1.5 * dot(u, u)) + 3.0 * dot(u, first) + 4.5 * dot(u, second)
    vector = [3.0 * first[a] + 9.0 * second[a] - 3.0 * (u[a] * total) for a in range(3)]
    return scalar - dot(vector, u), vector


def adjoint_back(m, rest, vector, kind, factor):
    omega = rates(kind)
    keep = 1.0 - omega
    wall = kind == 2
    rest = omega * rest
    scale = omega * factor
    turned = [scale * v for v in vector]
    out = [None] * 19
    out[0] = jnp.where(wall, m[0], keep * m[0] + rest)
    for i in PAIRS:
        c_v = along(i, turned)
        out[i] = jnp.where(wall, m[i + 1], keep * m[i] + (rest + c_v))
        out[i + 1] = jnp.where(wall, m[i], keep * m[i + 1] + (rest - c_v))
    return out


def gradient(vector, density, plain, kind):
    inner = vector[0] * plain[0] + vector[1] * plain[1] + vector[2] * plain[2]
    return jnp.where(kind == 2, 0.0, rates(kind) * density * inner)


def kernel(
    sizes,
    forward_hbm,
    later_hbm,
    design_hbm,
    kind_hbm,
    region_hbm,
    adjoint_hbm,
    sensitivity_hbm,
    objective_ref,
    volumes_ref,
    forward,
    kind,
    region,
    pops,
    fields,
    macro,
    factors,
    grads,
    result,
    smooth,
    x_send,
    x_recv,
    y_send,
    y_recv,
    c_send,
    c_recv,
    stat_y,
    stat_x,
    load_sem,
    send_sem,
    recv_sem,
    sum_send,
    sum_recv,
):
    count_x, count_y = sizes
    nx, ny = kind.shape[0], kind.shape[1]
    me_x, me_y = lax.axis_index("gx"), lax.axis_index("gy")
    halves = range(0, ny, ROWS)

    def device(dx, dy):
        return (
            lax.rem(me_x + dx + count_x, count_x),
            lax.rem(me_y + dy + count_y, count_y),
        )

    inner = (pl.ds(1, nx), pl.ds(ROWS, ny))
    loads = [
        pltpu.make_async_copy(
            design_hbm, fields.at[0, pl.ds(RAD, nx), pl.ds(ROWS, ny)], load_sem.at[0]
        ),
        pltpu.make_async_copy(later_hbm, pops.at[LATER, :, inner[0], inner[1]], load_sem.at[1]),
        pltpu.make_async_copy(forward_hbm, forward, load_sem.at[2]),
        pltpu.make_async_copy(kind_hbm, kind, load_sem.at[3]),
        pltpu.make_async_copy(region_hbm, region, load_sem.at[4]),
    ]
    for load in loads:
        load.start()

    partners = {((dx + count_x) % count_x, (dy + count_y) % count_y) for dx, dy in DIRS}
    partners |= {(0, k) for k in range(1, count_y)} | {(k, 0) for k in range(1, count_x)}
    barrier = pltpu.get_barrier_semaphore()
    for dx, dy in sorted(partners):
        pl.semaphore_signal(barrier, inc=1, device_id=device(dx, dy), device_id_type=MESH)
    loads[0].wait()
    pl.semaphore_wait(barrier, len(partners))

    def field_copies(slot, exchange):
        copies = []
        for j, (dx, dy) in enumerate(DIRS):
            width = nx if dx == 0 else RAD
            source_x = {0: RAD, 1: nx, -1: RAD}[dx]
            target_x = {0: RAD, 1: 0, -1: nx + RAD}[dx]
            height = ny if dy == 0 else ROWS
            source_y = {0: ROWS, 1: ny, -1: ROWS}[dy]
            target_y = {0: ROWS, 1: 0, -1: ny + ROWS}[dy]
            copies.append(
                pltpu.make_async_remote_copy(
                    src_ref=fields.at[slot, pl.ds(source_x, width), pl.ds(source_y, height)],
                    dst_ref=fields.at[slot, pl.ds(target_x, width), pl.ds(target_y, height)],
                    send_sem=send_sem.at[exchange, j],
                    recv_sem=recv_sem.at[exchange, j],
                    device_id=device(dx, dy),
                    device_id_type=MESH,
                )
            )
        return copies

    def pops_copies(slot):
        copies = []
        for j, direction in enumerate(DIRS):
            if direction[1] == 0:
                source, target, k = x_send, x_recv, j
            elif direction[0] == 0:
                source, target, k = y_send, y_recv, j - 2
            else:
                source, target, k = c_send, c_recv, j - 4
            copies.append(
                pltpu.make_async_remote_copy(
                    src_ref=source.at[slot, k],
                    dst_ref=target.at[slot, k],
                    send_sem=send_sem.at[slot, j],
                    recv_sem=recv_sem.at[slot, j],
                    device_id=device(*direction),
                    device_id_type=MESH,
                )
            )
        return copies

    def send_pops(slot, sign):
        copies = pops_copies(slot)
        for j, (dx, dy) in enumerate(DIRS):
            x = nx if dx == 1 else 1
            y = ROWS + ny - 1 if dy == 1 else ROWS
            for k, i in enumerate(crossing((dx, dy), sign)):
                if dy == 0:
                    x_send[slot, j, k] = pops[slot, i, x, ROWS : ROWS + ny, :]
                elif dx == 0:
                    for row in range(nx):
                        y_send[slot, j - 2, k, row : row + 1, :] = pops[
                            slot, i, row + 1, y : y + 1, :
                        ]
                else:
                    c_send[slot, j - 4] = pops[slot, i, x, y : y + 1, :]
            copies[j].start()
        return copies

    def take_pops(slot, sign, copies):
        for j, (dx, dy) in enumerate(DIRS):
            copies[j].wait_recv()
            x = 0 if dx == 1 else nx + 1
            y = ROWS - 1 if dy == 1 else ROWS + ny
            for k, i in enumerate(crossing((dx, dy), sign)):
                if dy == 0:
                    pops[slot, i, x, ROWS : ROWS + ny, :] = x_recv[slot, j, k]
                elif dx == 0:
                    for row in range(nx):
                        pops[slot, i, row + 1, y : y + 1, :] = y_recv[
                            slot, j - 2, k, row : row + 1, :
                        ]
                else:
                    pops[slot, i, x, y : y + 1, :] = c_recv[slot, j - 4]

    def pick(slot, i, x, y, sign):
        cx, cy, cz = (sign * c for c in VELOCITY[i])
        value = pops[slot, i, x + 1 + cx, ROWS + y + cy : 2 * ROWS + y + cy, :]
        return shifted(value, cz)

    design_copies = field_copies(0, DESIGN)
    for copy in design_copies:
        copy.start()
    loads[1].wait()
    later_copies = send_pops(LATER, -1)
    for load in loads[2:]:
        load.wait()

    def macroscopic(x, carry):
        for y in halves:
            density, momenta = moments([forward[i, x, y : y + ROWS, :] for i in range(19)])
            inverse = 1.0 / density
            macro[0, x, y : y + ROWS, :] = density
            for a in range(3):
                macro[a + 1, x, y : y + ROWS, :] = momenta[a] * inverse
        return carry

    lax.fori_loop(0, nx, macroscopic, 0)
    inv_norm = inverse_norm((ROWS, kind.shape[2]))
    for copy in design_copies:
        copy.wait_recv()

    def first_step(x, sums):
        sums = list(sums)
        for y in halves:
            rows = slice(y, y + ROWS)
            kinds = kind[x, rows, :]
            design_cell = kinds == 1
            filtered = filter_taps(fields.at[0], x, y) * inv_norm
            factor = jnp.where(design_cell, 1.0 - BRINKMAN * (1.0 - filtered), 1.0)
            factors[x, rows, :] = factor
            regions = region[x, rows, :]
            inside = jnp.where(design_cell, filtered, 0.0)
            for r in range(REG):
                sums[r] = sums[r] + jnp.where(regions == r, inside, 0.0)
            post = collide(
                [forward[i, x, rows, :] for i in range(19)],
                macro[0, x, rows, :],
                [macro[a + 1, x, rows, :] for a in range(3)],
                kinds,
                factor,
            )
            for i in range(19):
                pops[POST, i, x + 1, ROWS + y : 2 * ROWS + y, :] = post[i]
        return tuple(sums)

    zero = jnp.zeros((ROWS, kind.shape[2]), jnp.float32)
    volumes = lax.fori_loop(0, nx, first_step, (zero,) * REG)
    post_copies = send_pops(POST, 1)
    take_pops(LATER, -1, later_copies)
    take_pops(POST, 1, post_copies)

    def middle_step(x, total):
        for y in halves:
            rows = slice(y, y + ROWS)
            kinds = kind[x, rows, :]
            factor = factors[x, rows, :]
            density, momenta = moments([pick(POST, i, x, y, -1) for i in range(19)])
            outlet = kinds == 4
            total = total + jnp.where(outlet, momenta[0], 0.0)
            inverse = 1.0 / density
            plain = [m * inverse for m in momenta]
            incoming = [pick(LATER, i, x, y, 1) for i in range(19)]
            rest, vector = adjoint_parts(incoming, plain, factor)
            grads[x, rows, :] = gradient(vector, density, plain, kinds)
            middle = adjoint_back(incoming, rest, vector, kinds, factor)
            source = jnp.where(outlet, 1.0, 0.0)
            for i in range(19):
                value = middle[i]
                if VELOCITY[i][0] == 1:
                    value = value + source
                elif VELOCITY[i][0] == -1:
                    value = value - source
                pops[MIDDLE, i, x + 1, ROWS + y : 2 * ROWS + y, :] = value
        return total

    objective = lax.fori_loop(0, nx, middle_step, zero)
    middle_copies = send_pops(MIDDLE, -1)

    def spread(stat, count, me, sem, place):
        copies = []
        for k in range(1, count):
            copies.append(
                pltpu.make_async_remote_copy(
                    src_ref=stat.at[me],
                    dst_ref=stat.at[me],
                    send_sem=sum_send.at[sem, k],
                    recv_sem=sum_recv.at[sem, k],
                    device_id=place(k),
                    device_id_type=MESH,
                )
            )
        for copy in copies:
            copy.start()
        return copies

    for r in range(REG):
        stat_y[me_y, r : r + 1, :] = jnp.sum(volumes[r], axis=0, keepdims=True)
    stat_y[me_y, REG : REG + 1, :] = jnp.sum(objective, axis=0, keepdims=True)
    stat_y[me_y, REG + 1 :, :] = jnp.zeros((REG - 1, zero.shape[1]), jnp.float32)
    sums_y = spread(stat_y, count_y, me_y, 0, lambda k: device(0, k))
    take_pops(MIDDLE, -1, middle_copies)

    def second_step(x, carry):
        for y in halves:
            rows = slice(y, y + ROWS)
            kinds = kind[x, rows, :]
            factor = factors[x, rows, :]
            density = macro[0, x, rows, :]
            plain = [macro[a + 1, x, rows, :] for a in range(3)]
            incoming = [pick(MIDDLE, i, x, y, 1) for i in range(19)]
            rest, vector = adjoint_parts(incoming, plain, factor)
            grad = grads[x, rows, :] + gradient(vector, density, plain, kinds)
            raw = jnp.where(kinds == 1, BRINKMAN * grad, 0.0) * inv_norm
            fields[1, x + RAD, ROWS + y : 2 * ROWS + y, :] = raw
            back = adjoint_back(incoming, rest, vector, kinds, factor)
            for i in range(19):
                result[i, x, rows, :] = back[i]
        return carry

    lax.fori_loop(0, nx, second_step, 0)
    raw_copies = field_copies(1, RAW)
    for copy in raw_copies:
        copy.start()
    store = pltpu.make_async_copy(result, adjoint_hbm, load_sem.at[5])
    store.start()

    for copy in sums_y:
        copy.wait()
    subtotal = stat_y[0]
    for k in range(1, count_y):
        subtotal = subtotal + stat_y[k]
    stat_x[me_x] = subtotal
    sums_x = spread(stat_x, count_x, me_x, 1, lambda k: device(k, 0))
    for copy in raw_copies:
        copy.wait_recv()

    def last_step(x, carry):
        for y in halves:
            smooth[x, y : y + ROWS, :] = filter_taps(fields.at[1], x, y)
        return carry

    lax.fori_loop(0, nx, last_step, 0)
    store_smooth = pltpu.make_async_copy(smooth, sensitivity_hbm, load_sem.at[6])
    store_smooth.start()
    for copy in sums_x:
        copy.wait()
    total = stat_x[0]
    for k in range(1, count_x):
        total = total + stat_x[k]
    total = jnp.sum(total, axis=1, keepdims=True)
    for r in range(REG):
        volumes_ref[r] = total[r, 0]
    objective_ref[0] = total[REG, 0]
    for copies in (design_copies, later_copies, post_copies, middle_copies, raw_copies):
        for copy in copies:
            copy.wait_send()
    store.wait()
    store_smooth.wait()


def per_device(sizes, forward_pops, later_adjoint, design, node_type, region):
    nx, ny, nz = design.shape
    f32 = jnp.float32
    anywhere = pl.BlockSpec(memory_space=pl.ANY)
    scalars = pl.BlockSpec(memory_space=pltpu.SMEM)
    block = (nx, ny, nz)
    most = max(sizes)
    adjoint, sensitivity, objective, volumes = pl.pallas_call(
        functools.partial(kernel, sizes),
        out_shape=(
            jax.ShapeDtypeStruct((19,) + block, f32),
            jax.ShapeDtypeStruct(block, f32),
            jax.ShapeDtypeStruct((1,), f32),
            jax.ShapeDtypeStruct((REG,), f32),
        ),
        in_specs=[anywhere] * 5,
        out_specs=(anywhere, anywhere, scalars, scalars),
        scratch_shapes=[
            pltpu.VMEM((19,) + block, f32),
            pltpu.VMEM(block, jnp.int32),
            pltpu.VMEM(block, jnp.int32),
            pltpu.VMEM((3, 19, nx + 2, ny + 2 * ROWS, nz), f32),
            pltpu.VMEM((2, nx + 2 * RAD, ny + 2 * ROWS, nz), f32),
            pltpu.VMEM((4,) + block, f32),
            pltpu.VMEM(block, f32),
            pltpu.VMEM(block, f32),
            pltpu.VMEM((19,) + block, f32),
            pltpu.VMEM(block, f32),
            pltpu.VMEM((3, 2, 5, ny, nz), f32),
            pltpu.VMEM((3, 2, 5, ny, nz), f32),
            pltpu.VMEM((3, 2, 5, nx, nz), f32),
            pltpu.VMEM((3, 2, 5, nx, nz), f32),
            pltpu.VMEM((3, 4, 1, nz), f32),
            pltpu.VMEM((3, 4, 1, nz), f32),
            pltpu.VMEM((sizes[1], 2 * REG, nz), f32),
            pltpu.VMEM((sizes[0], 2 * REG, nz), f32),
            pltpu.SemaphoreType.DMA((7,)),
            pltpu.SemaphoreType.DMA((5, 8)),
            pltpu.SemaphoreType.DMA((5, 8)),
            pltpu.SemaphoreType.DMA((2, most)),
            pltpu.SemaphoreType.DMA((2, most)),
        ],
        compiler_params=pltpu.CompilerParams(
            collective_id=0, has_side_effects=True, vmem_limit_bytes=40 * 1024 * 1024
        ),
        name="lattice_adjoint",
    )(forward_pops, later_adjoint, design, node_type, region)
    return adjoint, sensitivity, objective.reshape(()), volumes


def solution(mesh):
    sizes = (mesh.shape["gx"], mesh.shape["gy"])
    in_specs = (
        P(None, "gx", "gy", None),
        P(None, "gx", "gy", None),
        P("gx", "gy", None),
        P("gx", "gy", None),
        P("gx", "gy", None),
    )
    out_specs = (P(None, "gx", "gy", None), P("gx", "gy", None), P(), P())
    return jax.shard_map(
        functools.partial(per_device, sizes),
        mesh=mesh,
        in_specs=in_specs,
        out_specs=out_specs,
        check_vma=False,
    )
```

time: 130 us -> 42.8 us (0.33)
  blocking collectives: 35.5 us -> 0 us
  Pallas kernels: 0 us -> 32.8 us
  waiting for transfers between devices: 32.5 us -> 0 us
  starting transfers between devices: 26.6 us -> 0 us
  other arithmetic: 25.4 us -> 0 us
    psum x1 -> x0, blocking collectives: 35.5 us -> none  [per_device(): objective, volumes = lax.psum((objective_local, volume_local), ('gx', 'gy'))]
    pallas_call x0 -> x1, Pallas kernels: none -> 32.8 us  [per_device(): pl.pallas_call(functools.partial(kernel, sizes), out_shape=(jax.ShapeDtyp...]
    ppermute x16 -> x0, waiting for transfers between devices: 32.5 us -> none  [the longest x8 20 us: padded_2(): lax.ppermute(lax.slice_in_dim(block, block.shape[dim] - width, None, axis...]
    ppermute x16 -> x0, starting transfers between devices: 26.6 us -> none  [the longest x8 13.3 us: padded_2(): lax.ppermute(lax.slice_in_dim(block, block.shape[dim] - width, None, axis...]
    concatenate x7 -> x0, other arithmetic: 7.36 us -> none  [padded_2(): block = jnp.concatenate([low, block, high], axis=dim)]
    unnamed x73 -> x0, other arithmetic: 6.69 us -> none
    unnamed x21 -> x13, local copies, waits for them, and re-layouts: 1.05 us -> 7.28 us
    another operation x13 -> x0, local copies, waits for them, and re-layouts: 5.78 us -> none  [the longest x1 5.7 us: per_device(): jnp.stack([jnp.sum(jnp.where((node_type == 1) & (region == r), filtered,...]
  transfers between devices with their start and end apart: 16 -> 0, of which waited for: 11 -> 0; matrix products, arithmetic and copies ran while one was open for 7% -> 0% of each run, Pallas kernels for 0% -> 0%
where the time goes in v1:
time: 42.8 us; the launch traced here: 42.4 us
  Pallas kernels  32.8 us (77%)
  local copies, waits for them, and re-layouts  7.28 us (17%)
  between operations  2.35 us (5%)
    pallas_call x1, Pallas kernels, per_device(): pl.pallas_call(functools.partial(kernel, sizes), out_shape=(jax.ShapeDtyp...  32.8 us
    unnamed x13, local copies, waits for them, and re-layouts  7.28 us

profile of v1, /device:TPU:1, one launch (start us, length us, event | category | flops | bytes accessed | tf_op | source)
XLA Modules:
  0.0 42.4 jit_solution(14438204262193935150)
XLA Ops:
  0.6 0.0 copy-start
  0.6 1.3 %copy-done = f32[19,8,16,128]{3,2,1,0:T(8,128)S(1)} copy-done((f32[19,8,16,128]{3,2,1,0:T(8,128)S(1)}, f32[19,8,16,128]{3,2,1,0:T(8,128)}, u32[]{:S(2)}) %copy-start) | copy-done | bytes 1245208
  1.9 0.0 copy-start.1
  1.9 1.3 %copy-done.1 = f32[19,8,16,128]{3,2,1,0:T(8,128)S(1)} copy-done((f32[19,8,16,128]{3,2,1,0:T(8,128)S(1)}, f32[19,8,16,128]{3,2,1,0:T(8,128)}, u32[]{:S(2)}) %copy-start.1) | copy-done | bytes 1245208
  3.2 0.0 copy-start.2
  3.2 0.8 %copy-done.2 = f32[8,16,128]{2,1,0:T(8,128)S(1)} copy-done((f32[8,16,128]{2,1,0:T(8,128)S(1)}, f32[8,16,128]{2,1,0:T(8,128)}, u32[]{:S(2)}) %copy-start.2) | copy-done | bytes 65560
  4.1 0.0 copy-start.3
  4.1 0.8 %copy-done.3 = s32[8,16,128]{2,1,0:T(8,128)S(1)} copy-done((s32[8,16,128]{2,1,0:T(8,128)S(1)}, s32[8,16,128]{2,1,0:T(8,128)}, u32[]{:S(2)}) %copy-start.3) | copy-done | bytes 65560
  4.9 0.0 copy-start.4
  4.9 0.8 %copy-done.4 = s32[8,16,128]{2,1,0:T(8,128)S(1)} copy-done((s32[8,16,128]{2,1,0:T(8,128)S(1)}, s32[8,16,128]{2,1,0:T(8,128)}, u32[]{:S(2)}) %copy-start.4) | copy-done | bytes 65560
  5.7 32.8 %lattice_adjoint.1 = (f32[19,8,16,128]{3,2,1,0:T(8,128)S(1)}, f32[8,16,128]{2,1,0:T(8,128)S(1)}, f32[1]{0:T(128)}, f32[8]{0:T(128)S(1)}) custom-call(f32[19,8,16,128]{3,2,1,0:T(8,128)S(1)} %copy-done, f32[19,8,16,128]{3,2,1,0:T(8,128)S(1)} %copy-done.1, f32[8,16,128]{2,1,0:T(8,128)S(1)} %copy-done.2, s32[8,16,128]{2,1,0:T(8,128)S(1)} %copy-done.3, ...), custom_call_target="tpu_custom_call" | custom-call | tf_op jit(solution)/shard_map/lattice_adjoint/pallas_call | solution.py:537
  38.5 1.0 %copy.13 = f32[19,8,16,128]{3,2,1,0:T(8,128)} copy(f32[19,8,16,128]{3,2,1,0:T(8,128)S(1)} %get-tuple-element.16) | data formatting | bytes 2490368
  39.6 0.6 %copy.14 = f32[8,16,128]{2,1,0:T(8,128)} copy(f32[8,16,128]{2,1,0:T(8,128)S(1)} %get-tuple-element.17) | data formatting | bytes 131072
  40.8 0.5 %copy.16 = f32[8]{0:T(128)} copy(f32[8]{0:T(128)S(1)} %get-tuple-element.19) | data formatting | bytes 64
Async XLA Ops:
  0.6 1.3 %copy-start = (f32[19,8,16,128]{3,2,1,0:T(8,128)S(1)}, f32[19,8,16,128]{3,2,1,0:T(8,128)}, u32[]{:S(2)}) copy-start(f32[19,8,16,128]{3,2,1,0:T(8,128)} %forward_hbm.1) | copy-start | bytes 3735556
  1.9 1.3 %copy-start.1 = (f32[19,8,16,128]{3,2,1,0:T(8,128)S(1)}, f32[19,8,16,128]{3,2,1,0:T(8,128)}, u32[]{:S(2)}) copy-start(f32[19,8,16,128]{3,2,1,0:T(8,128)} %later_hbm.1) | copy-start | bytes 3735556
  3.2 0.8 %copy-start.2 = (f32[8,16,128]{2,1,0:T(8,128)S(1)}, f32[8,16,128]{2,1,0:T(8,128)}, u32[]{:S(2)}) copy-start(f32[8,16,128]{2,1,0:T(8,128)} %design_hbm.1) | copy-start | bytes 196612
  4.1 0.8 %copy-start.3 = (s32[8,16,128]{2,1,0:T(8,128)S(1)}, s32[8,16,128]{2,1,0:T(8,128)}, u32[]{:S(2)}) copy-start(s32[8,16,128]{2,1,0:T(8,128)} %kind_hbm.1) | copy-start | bytes 196612
  4.9 0.8 %copy-start.4 = (s32[8,16,128]{2,1,0:T(8,128)S(1)}, s32[8,16,128]{2,1,0:T(8,128)}, u32[]{:S(2)}) copy-start(s32[8,16,128]{2,1,0:T(8,128)} %region_hbm.1) | copy-start | bytes 196612

commit v2 on v1

--- a/solution.py
+++ b/solution.py
@@ -570,7 +570,7 @@
             pltpu.SemaphoreType.DMA((2, most)),
         ],
         compiler_params=pltpu.CompilerParams(
-            collective_id=0, has_side_effects=True, vmem_limit_bytes=40 * 1024 * 1024
+            collective_id=0, has_side_effects=True, vmem_limit_bytes=60 * 1024 * 1024
         ),
         name="lattice_adjoint",
     )(forward_pops, later_adjoint, design, node_type, region)

time: 42.8 us -> 38.6 us (0.902)
  local copies, waits for them, and re-layouts: 7.28 us -> 3.62 us
    unnamed x13 -> x7, local copies, waits for them, and re-layouts: 7.28 us -> 3.62 us
where the time goes in v2:
time: 38.6 us; the launch traced here: 38.4 us
  Pallas kernels  32.4 us (84%)
  local copies, waits for them, and re-layouts  3.62 us (9%)
  between operations  2.37 us (6%)
    pallas_call x1, Pallas kernels, per_device(): pl.pallas_call(functools.partial(kernel, sizes), out_shape=(jax.ShapeDtyp...  32.4 us
    unnamed x7, local copies, waits for them, and re-layouts  3.62 us

profile of v2, /device:TPU:1, one launch (start us, length us, event | category | flops | bytes accessed | tf_op | source)
XLA Modules:
  0.0 38.4 jit_solution(17821362357553405552)
XLA Ops:
  0.6 32.4 %lattice_adjoint.1 = (f32[19,8,16,128]{3,2,1,0:T(8,128)}, f32[8,16,128]{2,1,0:T(8,128)}, f32[1]{0:T(128)}, f32[8]{0:T(128)}) custom-call(f32[19,8,16,128]{3,2,1,0:T(8,128)} %forward_hbm.1, f32[19,8,16,128]{3,2,1,0:T(8,128)} %later_hbm.1, f32[8,16,128]{2,1,0:T(8,128)} %design_hbm.1, s32[8,16,128]{2,1,0:T(8,128)} %kind_hbm.1, s32[8,16,128]{2,1,0:T(8,128)} %region_hbm.1), custom_call_target="tpu_custom_call" | custom-call | tf_op jit(solution)/shard_map/lattice_adjoint/pallas_call | solution.py:537
  33.0 0.0 copy-start
  33.1 0.0 copy-start.1
  33.1 2.5 %copy.13 = f32[19,8,16,128]{3,2,1,0:T(8,128)} copy(f32[19,8,16,128]{3,2,1,0:T(8,128)} %get-tuple-element.16) | data formatting | bytes 2490368
  35.5 0.0 copy-done
  35.5 0.6 %copy.14 = f32[8,16,128]{2,1,0:T(8,128)} copy(f32[8,16,128]{2,1,0:T(8,128)S(1)} %copy-done) | data formatting | bytes 131072
  36.7 0.0 copy-done.1
  36.8 0.5 %copy.16 = f32[8]{0:T(128)} copy(f32[8]{0:T(128)S(1)} %copy-done.1) | data formatting | bytes 64
Async XLA Ops:
  33.0 2.5 %copy-start = (f32[8,16,128]{2,1,0:T(8,128)S(1)}, f32[8,16,128]{2,1,0:T(8,128)}, u32[]{:S(2)}) copy-start(f32[8,16,128]{2,1,0:T(8,128)} %get-tuple-element.17) | copy-start | bytes 196612
  33.1 3.7 %copy-start.1 = (f32[8]{0:T(128)S(1)}, f32[8]{0:T(128)}, u32[]{:S(2)}) copy-start(f32[8]{0:T(128)} %get-tuple-element.19) | copy-start | bytes 100

commit v3 on v2

--- a/solution.py
+++ b/solution.py
@@ -40,6 +40,8 @@
 BRINKMAN = 0.9
 
 DIRS = [(1, 0), (-1, 0), (0, 1), (0, -1), (1, 1), (-1, -1), (1, -1), (-1, 1)]
+ALONG_Y = [2, 3]
+ACROSS_X = [0, 1, 4, 5, 6, 7]
 ROWS = 8
 POST, LATER, MIDDLE = 0, 1, 2
 DESIGN, RAW = 3, 4
@@ -264,6 +266,12 @@
             lax.rem(me_y + dy + count_y, count_y),
         )
 
+    def rim_planes(body, carry):
+        return lax.fori_loop(0, 2, lambda k, c: body(k * (nx - 1), c), carry)
+
+    def inner_planes(body, carry):
+        return lax.fori_loop(1, nx - 1, body, carry)
+
     inner = (pl.ds(1, nx), pl.ds(ROWS, ny))
     loads = [
         pltpu.make_async_copy(
@@ -327,9 +335,9 @@
             )
         return copies
 
-    def send_pops(slot, sign):
-        copies = pops_copies(slot)
-        for j, (dx, dy) in enumerate(DIRS):
+    def send_pops(slot, sign, copies, which):
+        for j in which:
+            dx, dy = DIRS[j]
             x = nx if dx == 1 else 1
             y = ROWS + ny - 1 if dy == 1 else ROWS
             for k, i in enumerate(crossing((dx, dy), sign)):
@@ -343,10 +351,10 @@
                 else:
                     c_send[slot, j - 4] = pops[slot, i, x, y : y + 1, :]
             copies[j].start()
-        return copies
-
-    def take_pops(slot, sign, copies):
-        for j, (dx, dy) in enumerate(DIRS):
+
+    def take_pops(slot, sign, copies, which):
+        for j in which:
+            dx, dy = DIRS[j]
             copies[j].wait_recv()
             x = 0 if dx == 1 else nx + 1
             y = ROWS - 1 if dy == 1 else ROWS + ny
@@ -370,7 +378,8 @@
     for copy in design_copies:
         copy.start()
     loads[1].wait()
-    later_copies = send_pops(LATER, -1)
+    later_copies = pops_copies(LATER)
+    send_pops(LATER, -1, later_copies, ACROSS_X + ALONG_Y)
     for load in loads[2:]:
         load.wait()
 
@@ -413,10 +422,13 @@
         return tuple(sums)
 
     zero = jnp.zeros((ROWS, kind.shape[2]), jnp.float32)
-    volumes = lax.fori_loop(0, nx, first_step, (zero,) * REG)
-    post_copies = send_pops(POST, 1)
-    take_pops(LATER, -1, later_copies)
-    take_pops(POST, 1, post_copies)
+    post_copies = pops_copies(POST)
+    volumes = rim_planes(first_step, (zero,) * REG)
+    send_pops(POST, 1, post_copies, ACROSS_X)
+    volumes = inner_planes(first_step, volumes)
+    send_pops(POST, 1, post_copies, ALONG_Y)
+    take_pops(LATER, -1, later_copies, ALONG_Y + ACROSS_X)
+    take_pops(POST, 1, post_copies, ALONG_Y)
 
     def middle_step(x, total):
         for y in halves:
@@ -442,8 +454,11 @@
                 pops[MIDDLE, i, x + 1, ROWS + y : 2 * ROWS + y, :] = value
         return total
 
-    objective = lax.fori_loop(0, nx, middle_step, zero)
-    middle_copies = send_pops(MIDDLE, -1)
+    objective = inner_planes(middle_step, zero)
+    take_pops(POST, 1, post_copies, ACROSS_X)
+    objective = rim_planes(middle_step, objective)
+    middle_copies = pops_copies(MIDDLE)
+    send_pops(MIDDLE, -1, middle_copies, ACROSS_X + ALONG_Y)
 
     def spread(stat, count, me, sem, place):
         copies = []
@@ -467,7 +482,7 @@
     stat_y[me_y, REG : REG + 1, :] = jnp.sum(objective, axis=0, keepdims=True)
     stat_y[me_y, REG + 1 :, :] = jnp.zeros((REG - 1, zero.shape[1]), jnp.float32)
     sums_y = spread(stat_y, count_y, me_y, 0, lambda k: device(0, k))
-    take_pops(MIDDLE, -1, middle_copies)
+    take_pops(MIDDLE, -1, middle_copies, ALONG_Y)
 
     def second_step(x, carry):
         for y in halves:
@@ -486,7 +501,9 @@
                 result[i, x, rows, :] = back[i]
         return carry
 
-    lax.fori_loop(0, nx, second_step, 0)
+    inner_planes(second_step, 0)
+    take_pops(MIDDLE, -1, middle_copies, ACROSS_X)
+    rim_planes(second_step, 0)
     raw_copies = field_copies(1, RAW)
     for copy in raw_copies:
         copy.start()

time: 38.6 us -> 35.7 us (0.925)
  Pallas kernels: 32.4 us -> 29.5 us
    pallas_call x1, Pallas kernels: 32.4 us -> 29.5 us  [per_device(): pl.pallas_call(functools.partial(kernel, sizes), out_shape=(jax.ShapeDtyp...]
where the time goes in v3:
time: 35.7 us; the launch traced here: 35.5 us
  Pallas kernels  29.5 us (83%)
  local copies, waits for them, and re-layouts  3.62 us (10%)
  between operations  2.37 us (7%)
    pallas_call x1, Pallas kernels, per_device(): pl.pallas_call(functools.partial(kernel, sizes), out_shape=(jax.ShapeDtyp...  29.5 us
    unnamed x7, local copies, waits for them, and re-layouts  3.62 us

profile of v3, /device:TPU:1, one launch (start us, length us, event | category | flops | bytes accessed | tf_op | source)
XLA Modules:
  0.0 35.5 jit_solution(9933060566625922395)
XLA Ops:
  0.6 29.5 %lattice_adjoint.1 = (f32[19,8,16,128]{3,2,1,0:T(8,128)}, f32[8,16,128]{2,1,0:T(8,128)}, f32[1]{0:T(128)}, f32[8]{0:T(128)}) custom-call(f32[19,8,16,128]{3,2,1,0:T(8,128)} %forward_hbm.1, f32[19,8,16,128]{3,2,1,0:T(8,128)} %later_hbm.1, f32[8,16,128]{2,1,0:T(8,128)} %design_hbm.1, s32[8,16,128]{2,1,0:T(8,128)} %kind_hbm.1, s32[8,16,128]{2,1,0:T(8,128)} %region_hbm.1), custom_call_target="tpu_custom_call" | custom-call | tf_op jit(solution)/shard_map/lattice_adjoint/pallas_call | solution.py:554
  30.2 0.0 copy-start
  30.2 0.0 copy-start.1
  30.2 2.5 %copy.13 = f32[19,8,16,128]{3,2,1,0:T(8,128)} copy(f32[19,8,16,128]{3,2,1,0:T(8,128)} %get-tuple-element.16) | data formatting | bytes 2490368
  32.7 0.0 copy-done
  32.7 0.6 %copy.14 = f32[8,16,128]{2,1,0:T(8,128)} copy(f32[8,16,128]{2,1,0:T(8,128)S(1)} %copy-done) | data formatting | bytes 131072
  33.9 0.0 copy-done.1
  33.9 0.5 %copy.16 = f32[8]{0:T(128)} copy(f32[8]{0:T(128)S(1)} %copy-done.1) | data formatting | bytes 64
Async XLA Ops:
  30.2 2.5 %copy-start = (f32[8,16,128]{2,1,0:T(8,128)S(1)}, f32[8,16,128]{2,1,0:T(8,128)}, u32[]{:S(2)}) copy-start(f32[8,16,128]{2,1,0:T(8,128)} %get-tuple-element.17) | copy-start | bytes 196612
  30.2 3.7 %copy-start.1 = (f32[8]{0:T(128)S(1)}, f32[8]{0:T(128)}, u32[]{:S(2)}) copy-start(f32[8]{0:T(128)} %get-tuple-element.19) | copy-start | bytes 100

commit v4 on v3

--- a/solution.py
+++ b/solution.py
@@ -229,8 +229,7 @@
     region_hbm,
     adjoint_hbm,
     sensitivity_hbm,
-    objective_ref,
-    volumes_ref,
+    stats_ref,
     forward,
     kind,
     region,
@@ -533,15 +532,42 @@
     total = stat_x[0]
     for k in range(1, count_x):
         total = total + stat_x[k]
-    total = jnp.sum(total, axis=1, keepdims=True)
-    for r in range(REG):
-        volumes_ref[r] = total[r, 0]
-    objective_ref[0] = total[REG, 0]
+    stats_ref[...] = total
     for copies in (design_copies, later_copies, post_copies, middle_copies, raw_copies):
         for copy in copies:
             copy.wait_send()
     store.wait()
     store_smooth.wait()
+
+
+def finish(
+    adjoint_in,
+    sensitivity_in,
+    stats_in,
+    adjoint_out,
+    sensitivity_out,
+    objective_ref,
+    volumes_ref,
+    stats,
+    sem,
+):
+    load = pltpu.make_async_copy(stats_in, stats, sem.at[0])
+    load.start()
+    count = adjoint_in.shape[0]
+    copies = [
+        pltpu.make_async_copy(adjoint_in.at[i], adjoint_out.at[i], sem.at[2 + i])
+        for i in range(count)
+    ]
+    copies.append(pltpu.make_async_copy(sensitivity_in, sensitivity_out, sem.at[1]))
+    for copy in copies:
+        copy.start()
+    load.wait()
+    total = jnp.sum(stats[...], axis=1, keepdims=True)
+    for r in range(REG):
+        volumes_ref[r] = total[r, 0]
+    objective_ref[0] = total[REG, 0]
+    for copy in copies:
+        copy.wait()
 
 
 def per_device(sizes, forward_pops, later_adjoint, design, node_type, region):
@@ -551,16 +577,15 @@
     scalars = pl.BlockSpec(memory_space=pltpu.SMEM)
     block = (nx, ny, nz)
     most = max(sizes)
-    adjoint, sensitivity, objective, volumes = pl.pallas_call(
+    adjoint, sensitivity, stats = pl.pallas_call(
         functools.partial(kernel, sizes),
         out_shape=(
             jax.ShapeDtypeStruct((19,) + block, f32),
             jax.ShapeDtypeStruct(block, f32),
-            jax.ShapeDtypeStruct((1,), f32),
-            jax.ShapeDtypeStruct((REG,), f32),
+            jax.ShapeDtypeStruct((2 * REG, nz), f32),
         ),
         in_specs=[anywhere] * 5,
-        out_specs=(anywhere, anywhere, scalars, scalars),
+        out_specs=(anywhere, anywhere, pl.BlockSpec(memory_space=pltpu.VMEM)),
         scratch_shapes=[
             pltpu.VMEM((19,) + block, f32),
             pltpu.VMEM(block, jnp.int32),
@@ -591,6 +616,23 @@
         ),
         name="lattice_adjoint",
     )(forward_pops, later_adjoint, design, node_type, region)
+    adjoint, sensitivity, objective, volumes = pl.pallas_call(
+        finish,
+        out_shape=(
+            jax.ShapeDtypeStruct((19,) + block, f32),
+            jax.ShapeDtypeStruct(block, f32),
+            jax.ShapeDtypeStruct((1,), f32),
+            jax.ShapeDtypeStruct((REG,), f32),
+        ),
+        in_specs=[anywhere] * 3,
+        out_specs=(anywhere, anywhere, scalars, scalars),
+        scratch_shapes=[
+            pltpu.VMEM((2 * REG, nz), f32),
+            pltpu.SemaphoreType.DMA((21,)),
+        ],
+        compiler_params=pltpu.CompilerParams(vmem_limit_bytes=60 * 1024 * 1024),
+        name="place_results",
+    )(adjoint, sensitivity, stats)
     return adjoint, sensitivity, objective.reshape(()), volumes
 
 

time: 35.7 us -> 72 us (2.02)
  Pallas kernels: 29.5 us -> 71.1 us
  local copies, waits for them, and re-layouts: 3.62 us -> 0 us
  between operations: 2.37 us -> 0.64 us
    pallas_call x0 -> x1, Pallas kernels: none -> 41.5 us  [per_device(): pl.pallas_call(finish, out_shape=(jax.ShapeDtypeStruct((19,) + block, f32...]
    unnamed x7 -> x0, local copies, waits for them, and re-layouts: 3.62 us -> none
where the time goes in v4:
time: 72 us; the launch traced here: 71.8 us
  Pallas kernels  71.1 us (99%)
    pallas_call x1, Pallas kernels, per_device(): pl.pallas_call(finish, out_shape=(jax.ShapeDtypeStruct((19,) + block, f32...  41.5 us
    pallas_call x1, Pallas kernels, per_device(): pl.pallas_call(functools.partial(kernel, sizes), out_shape=(jax.ShapeDtyp...  29.6 us

profile of v4, /device:TPU:1, one launch (start us, length us, event | category | flops | bytes accessed | tf_op | source)
XLA Modules:
  0.0 71.8 jit_solution(5128093481396842330)
XLA Ops:
  0.6 29.6 %lattice_adjoint.1 = (f32[19,8,16,128]{3,2,1,0:T(8,128)}, f32[8,16,128]{2,1,0:T(8,128)}, f32[16,128]{1,0:T(8,128)}) custom-call(f32[19,8,16,128]{3,2,1,0:T(8,128)} %forward_hbm.1, f32[19,8,16,128]{3,2,1,0:T(8,128)} %later_hbm.1, f32[8,16,128]{2,1,0:T(8,128)} %design_hbm.1, s32[8,16,128]{2,1,0:T(8,128)} %kind_hbm.1, s32[8,16,128]{2,1,0:T(8,128)} %region_hbm.1), custom_call_target="tpu_custom_call" | custom-call | tf_op jit(solution)/shard_map/lattice_adjoint/pallas_call | solution.py:580
  30.3 41.5 %place_results.1 = (f32[19,8,16,128]{3,2,1,0:T(8,128)}, f32[8,16,128]{2,1,0:T(8,128)}, f32[1]{0:T(128)}, f32[8]{0:T(128)}) custom-call(f32[19,8,16,128]{3,2,1,0:T(8,128)} %get-tuple-element.11.adjoint_in, f32[8,16,128]{2,1,0:T(8,128)} %get-tuple-element.12.sensitivity_in, f32[16,128]{1,0:T(8,128)} %get-tuple-element.13.stats_in), custom_call_target="tpu_custom_call" | custom-call | tf_op jit(solution)/shard_map/place_results/pallas_call | solution.py:619

commit v5 on v4

--- a/solution.py
+++ b/solution.py
@@ -549,17 +549,26 @@
     objective_ref,
     volumes_ref,
     stats,
+    held,
+    smooth,
     sem,
 ):
     load = pltpu.make_async_copy(stats_in, stats, sem.at[0])
     load.start()
-    count = adjoint_in.shape[0]
+    ways = [(adjoint_in.at[i], held.at[i], adjoint_out.at[i]) for i in range(19)]
+    ways.append((sensitivity_in, smooth, sensitivity_out))
+    loads = [
+        pltpu.make_async_copy(way[0], way[1], sem.at[1 + k])
+        for k, way in enumerate(ways)
+    ]
     copies = [
-        pltpu.make_async_copy(adjoint_in.at[i], adjoint_out.at[i], sem.at[2 + i])
-        for i in range(count)
+        pltpu.make_async_copy(way[1], way[2], sem.at[21 + k])
+        for k, way in enumerate(ways)
     ]
-    copies.append(pltpu.make_async_copy(sensitivity_in, sensitivity_out, sem.at[1]))
-    for copy in copies:
+    for copy in loads:
+        copy.start()
+    for arrival, copy in zip(loads, copies):
+        arrival.wait()
         copy.start()
     load.wait()
     total = jnp.sum(stats[...], axis=1, keepdims=True)
@@ -628,7 +637,9 @@
         out_specs=(anywhere, anywhere, scalars, scalars),
         scratch_shapes=[
             pltpu.VMEM((2 * REG, nz), f32),
-            pltpu.SemaphoreType.DMA((21,)),
+            pltpu.VMEM((19,) + block, f32),
+            pltpu.VMEM(block, f32),
+            pltpu.SemaphoreType.DMA((41,)),
         ],
         compiler_params=pltpu.CompilerParams(vmem_limit_bytes=60 * 1024 * 1024),
         name="place_results",

time: 72 us -> 33.3 us (0.46)
  Pallas kernels: 71.1 us -> 32.5 us
    pallas_call x1, Pallas kernels: 41.5 us -> 2.86 us  [per_device(): pl.pallas_call(finish, out_shape=(jax.ShapeDtypeStruct((19,) + block, f32...]
where the time goes in v5:
time: 33.3 us; the launch traced here: 33.1 us
  Pallas kernels  32.5 us (98%)
  between operations  0.64 us (2%)
    pallas_call x1, Pallas kernels, per_device(): pl.pallas_call(functools.partial(kernel, sizes), out_shape=(jax.ShapeDtyp...  29.6 us
    pallas_call x1, Pallas kernels, per_device(): pl.pallas_call(finish, out_shape=(jax.ShapeDtypeStruct((19,) + block, f32...  2.86 us

profile of v5, /device:TPU:1, one launch (start us, length us, event | category | flops | bytes accessed | tf_op | source)
XLA Modules:
  0.0 33.1 jit_solution(9534551518586710735)
XLA Ops:
  0.6 29.6 %lattice_adjoint.1 = (f32[19,8,16,128]{3,2,1,0:T(8,128)}, f32[8,16,128]{2,1,0:T(8,128)}, f32[16,128]{1,0:T(8,128)}) custom-call(f32[19,8,16,128]{3,2,1,0:T(8,128)} %forward_hbm.1, f32[19,8,16,128]{3,2,1,0:T(8,128)} %later_hbm.1, f32[8,16,128]{2,1,0:T(8,128)} %design_hbm.1, s32[8,16,128]{2,1,0:T(8,128)} %kind_hbm.1, s32[8,16,128]{2,1,0:T(8,128)} %region_hbm.1), custom_call_target="tpu_custom_call" | custom-call | tf_op jit(solution)/shard_map/lattice_adjoint/pallas_call | solution.py:589
  30.3 2.9 %place_results.1 = (f32[19,8,16,128]{3,2,1,0:T(8,128)}, f32[8,16,128]{2,1,0:T(8,128)}, f32[1]{0:T(128)}, f32[8]{0:T(128)}) custom-call(f32[19,8,16,128]{3,2,1,0:T(8,128)} %get-tuple-element.11.adjoint_in, f32[8,16,128]{2,1,0:T(8,128)} %get-tuple-element.12.sensitivity_in, f32[16,128]{1,0:T(8,128)} %get-tuple-element.13.stats_in), custom_call_target="tpu_custom_call" | custom-call | tf_op jit(solution)/shard_map/place_results/pallas_call | solution.py:628

commit v6 on v5

--- a/solution.py
+++ b/solution.py
@@ -501,6 +501,13 @@
         return carry
 
     inner_planes(second_step, 0)
+    for copy in sums_y:
+        copy.wait()
+    subtotal = stat_y[0]
+    for k in range(1, count_y):
+        subtotal = subtotal + stat_y[k]
+    stat_x[me_x] = subtotal
+    sums_x = spread(stat_x, count_x, me_x, 1, lambda k: device(k, 0))
     take_pops(MIDDLE, -1, middle_copies, ACROSS_X)
     rim_planes(second_step, 0)
     raw_copies = field_copies(1, RAW)
@@ -509,13 +516,6 @@
     store = pltpu.make_async_copy(result, adjoint_hbm, load_sem.at[5])
     store.start()
 
-    for copy in sums_y:
-        copy.wait()
-    subtotal = stat_y[0]
-    for k in range(1, count_y):
-        subtotal = subtotal + stat_y[k]
-    stat_x[me_x] = subtotal
-    sums_x = spread(stat_x, count_x, me_x, 1, lambda k: device(k, 0))
     for copy in raw_copies:
         copy.wait_recv()
 

time: 33.3 us -> 33.1 us (level)
  no operation moved by 1% of the time
where the time goes in v6:
time: 33.1 us; the launch traced here: 32.9 us
  Pallas kernels  32.2 us (97%)
  between operations  0.64 us (2%)
    pallas_call x1, Pallas kernels, per_device(): pl.pallas_call(functools.partial(kernel, sizes), out_shape=(jax.ShapeDtyp...  29.4 us
    pallas_call x1, Pallas kernels, per_device(): pl.pallas_call(finish, out_shape=(jax.ShapeDtypeStruct((19,) + block, f32...  2.86 us

profile of v6, /device:TPU:1, one launch (start us, length us, event | category | flops | bytes accessed | tf_op | source)
XLA Modules:
  0.0 32.9 jit_solution(8611387659610494015)
XLA Ops:
  0.6 29.4 %lattice_adjoint.1 = (f32[19,8,16,128]{3,2,1,0:T(8,128)}, f32[8,16,128]{2,1,0:T(8,128)}, f32[16,128]{1,0:T(8,128)}) custom-call(f32[19,8,16,128]{3,2,1,0:T(8,128)} %forward_hbm.1, f32[19,8,16,128]{3,2,1,0:T(8,128)} %later_hbm.1, f32[8,16,128]{2,1,0:T(8,128)} %design_hbm.1, s32[8,16,128]{2,1,0:T(8,128)} %kind_hbm.1, s32[8,16,128]{2,1,0:T(8,128)} %region_hbm.1), custom_call_target="tpu_custom_call" | custom-call | tf_op jit(solution)/shard_map/lattice_adjoint/pallas_call | solution.py:589
  30.0 2.9 %place_results.1 = (f32[19,8,16,128]{3,2,1,0:T(8,128)}, f32[8,16,128]{2,1,0:T(8,128)}, f32[1]{0:T(128)}, f32[8]{0:T(128)}) custom-call(f32[19,8,16,128]{3,2,1,0:T(8,128)} %get-tuple-element.11.adjoint_in, f32[8,16,128]{2,1,0:T(8,128)} %get-tuple-element.12.sensitivity_in, f32[16,128]{1,0:T(8,128)} %get-tuple-element.13.stats_in), custom_call_target="tpu_custom_call" | custom-call | tf_op jit(solution)/shard_map/place_results/pallas_call | solution.py:628
